TPU v7x, 512 devices: a whole 4x8x8 slice. The times are simulated.
512 devices in a mesh: ab: 4 (over x), ij: 16 (over y, core), cd: 8 (over z).
Axes of the slice: x: 4, y: 8, z: 8, core: 2. Of those that a mesh axis runs over, the one named last changes fastest.
Arguments:
- integrals: bfloat16 [1536, 163840], P('ab', ('cd', 'ij')), may hold values from -0.015625 to 0.015625
- amplitudes: bfloat16 [163840, 2048], P(('cd', 'ij'), 'ab'), may hold values from -24 to 24
Outputs:
- ladder: bfloat16 [1536, 2048], P(('ab', 'cd'), 'ij')
All inputs are finite; a program needn't handle non-finite values.
Results may differ from a plain program's by a relative error of at most 0.0012.
Values may be sent and summed in bfloat16 or wider, within the bound.
A program may use at most 64 MiB of HBM per device.

v0:
```python
import jax
import jax.numpy as jnp
from jax import lax
from jax.sharding import PartitionSpec as P


def per_device(integrals, amplitudes):
    partial_sums = jnp.dot(
        integrals,
        lax.all_gather(amplitudes, "ab", axis=1, tiled=True),
        preferred_element_type=jnp.float32,
    )
    reduced = lax.psum_scatter(partial_sums, "ij", scatter_dimension=1, tiled=True)
    reduced = lax.psum_scatter(reduced, "cd", scatter_dimension=0, tiled=True)
    return reduced.astype(jnp.bfloat16)


def solution(mesh):
    placed = (P("ab", ("cd", "ij")), P(("cd", "ij"), "ab"))
    return jax.shard_map(
        per_device, mesh=mesh, in_specs=placed, out_specs=P(("ab", "cd"), "ij"), check_vma=False
    )
```

profile of v0, /device:TPU:6, one launch (start us, length us, event | category | flops | bytes accessed | tf_op | source)
XLA Modules:
  0.0 196.3 jit_solution(14696364139880274659)
XLA Ops:
  6.5 0.0 copy-start
  6.5 0.0 all-gather.2.cloned.1.call-start
  6.5 0.7 all-gather.2.cloned.1.call-update
  7.3 0.0 reduce-scatter.3.cloned.1.call-start
  7.3 67.5 %all-gather.2.cloned.1.call-done = bf16[1280,2048]{1,0:T(8,128)(2,1)} async-done(((bf16[1280,512]{1,0:T(8,128)(2,1)}), bf16[1280,2048]{1,0:T(8,128)(2,1)}) %all-gather.2.cloned.1.call-update) | async-done | bytes 5242896 | tf_op jit(solution)/shard_map/all_gather | solution.py:10
  74.8 0.0 copy-done
  74.8 6.3 %fusion = f32[384,2048]{1,0:T(8,128)} fusion(bf16[384,1280]{1,0:T(8,128)(2,1)S(1)} %copy-done, bf16[1280,2048]{1,0:T(8,128)(2,1)} %all-gather.2.cloned.1.call-done), kind=kOutput, calls=%fused_computation | convolution fusion | flops 2013265920 | bytes 9371648 | tf_op jit(solution)/shard_map/dot_general | solution.py:8
  81.1 0.0 reduce-scatter.3.cloned.1.call-update
  81.1 0.0 reduce-scatter.5.cloned.1.call-start
  81.2 65.6 %reduce-scatter.3.cloned.1.call-done = f32[384,128]{1,0:T(8,128)} async-done(((f32[384,2048]{1,0:T(8,128)}), f32[384,128]{1,0:T(8,128)}) %reduce-scatter.3.cloned.1.call-update) | async-done | bytes 196624 | tf_op jit(solution)/shard_map/reduce_scatter | solution.py:13
  146.7 0.0 reduce-scatter.5.cloned.1.call-update
  146.8 41.7 %reduce-scatter.5.cloned.1.call-done = f32[48,128]{1,0:T(8,128)} async-done(((f32[384,128]{1,0:T(8,128)}), f32[48,128]{1,0:T(8,128)}) %reduce-scatter.5.cloned.1.call-update) | async-done | bytes 24592 | tf_op jit(solution)/shard_map/reduce_scatter | solution.py:14
  188.5 1.3 convert_element_type.3
Async XLA Ops:
  6.5 68.2 %copy-start = (bf16[384,1280]{1,0:T(8,128)(2,1)S(1)}, bf16[384,1280]{1,0:T(8,128)(2,1)}, u32[]{:S(2)}) copy-start(bf16[384,1280]{1,0:T(8,128)(2,1)} %param.2) | copy-start | bytes 2949124
  6.5 68.2 %all-gather.2.cloned.1.call-start = ((), (), s32[]{:S(2)}) async-start(), calls=%async_computation.2 | async-start | bytes 6553600 | tf_op jit(solution)/shard_map/all_gather | solution.py:10
  7.3 139.5 %reduce-scatter.3.cloned.1.call-start = ((), (), s32[]{:S(2)}) async-start(), calls=%async_computation.3 | async-start | bytes 3342336 | tf_op jit(solution)/shard_map/reduce_scatter | solution.py:13
  81.1 107.3 %reduce-scatter.5.cloned.1.call-start = ((), (), s32[]{:S(2)}) async-start(), calls=%async_computation.4 | async-start | bytes 221184 | tf_op jit(solution)/shard_map/reduce_scatter | solution.py:14
Sparse Core Ops, SparseCore 0:
  9.5 65.2 all-gather.1
  81.2 65.4 reduce-scatter.2
  149.5 38.8 reduce-scatter.4
where the time goes:
time: 197 us; the launch traced here: 196 us
  waiting for transfers between devices  175 us (89%)
  between operations  13.1 us (7%)
  matrix products  6.33 us (3%)
    all_gather x1, waiting for transfers between devices, per_device(): lax.all_gather(amplitudes, 'ab', axis=1, tiled=True)  67.5 us
    reduce_scatter x1, waiting for transfers between devices, per_device(): lax.psum_scatter(partial_sums, 'ij', scatter_dimension=1, tiled=True)  65.6 us
    reduce_scatter x1, waiting for transfers between devices, per_device(): reduced = lax.psum_scatter(reduced, 'cd', scatter_dimension=0, tiled=True)  41.7 us
    dot_general x1, matrix products, per_device(): jnp.dot(integrals, lax.all_gather(amplitudes, 'ab', axis=1, tiled=True),...  6.33 us
  transfers between devices with their start and end apart: 3, of which 3 were waited for; matrix products, arithmetic and copies ran while one was open for 0% of the time, Pallas kernels for 0%

commit v1 on v0

v1 whole, which is shorter than its diff:
```python
import jax
import jax.numpy as jnp
from jax import lax
from jax.experimental import pallas as pl
from jax.experimental.pallas import tpu as pltpu
from jax.sharding import PartitionSpec as P

MESH = pl.DeviceIdType.MESH
F32 = jnp.float32
BF16 = jnp.bfloat16
ROWS, DEPTH, COLS = 384, 1280, 512
N = 8
G = 48
W = 128


def kernel(v_hbm, t_hbm, out, v, t, p, sib, held, s1, r1, s2, fin,
           load_sem, xs_sem, xr_sem, cs_sem, cr_sem, s1s_sem, s1r_sem, s2s_sem, s2r_sem, fs_sem, fr_sem):
    x, ij, z = lax.axis_index("ab"), lax.axis_index("ij"), lax.axis_index("cd")
    y, c = ij // 2, ij % 2
    xv, xt = x + 1 - 2 * (x % 2), 3 - x
    me1 = z + c * (y - z)
    me2 = y + c * (z - y)

    def at(xx, ii, zz):
        return {"ab": xx, "ij": ii, "cd": zz}

    def first(q):
        return at(x, 2 * (y + c * (q - y)) + c, z + (1 - c) * (q - z))

    def second(q):
        return at(x, 2 * (y + (1 - c) * (q - y)) + c, z + c * (q - z))

    twin = at(x, ij + 1 - 2 * c, z)

    s_mine = me2 // 4
    j_mine = 2 * (me2 % 4) + c + s_mine * (1 - 2 * c)
    owner_x = x + s_mine * (xv - x)
    owner_ij = 4 * (x + (j_mine // 4) * (xt - x)) + j_mine % 4
    owner_is_me = (owner_x == x) & (owner_ij == ij) & (me1 == z)

    slab = ij // 4
    near = (slab == x) | (slab == 3 - x)
    src_s = jnp.where(near, 0, 1)
    src_x = x + src_s * (xv - x)
    src_j = jnp.where(slab == src_x, 0, 4) + ij % 4
    src_c = (src_s + src_j) % 2
    src_q = 4 * src_s + src_j // 2
    src_y = src_q + src_c * (z - src_q)
    src_z = z + src_c * (src_q - z)
    src_ij = 2 * src_y + src_c

    barrier = pltpu.get_barrier_semaphore()

    def greet(device):
        pl.semaphore_signal(barrier, inc=1, device_id=device, device_id_type=MESH)

    greet(at(xv, ij, z))
    greet(at(xt, ij, z))
    greet(twin)
    for d in range(1, N):
        greet(first((me1 + d) % N))
        greet(second((me2 + d) % N))

    @pl.when(jnp.logical_not(owner_is_me))
    def _():
        greet(at(owner_x, owner_ij, me1))
        greet(at(src_x, src_ij, src_z))

    load_v = pltpu.make_async_copy(v_hbm, v.at[0], load_sem.at[0])
    load_t = pltpu.make_async_copy(t_hbm, t.at[:, pl.ds(0, COLS)], load_sem.at[1])
    load_v.start()
    load_t.start()

    @pl.when(jnp.logical_not(owner_is_me))
    def _():
        pl.semaphore_wait(barrier, 5 + 2 * (N - 1))

    @pl.when(owner_is_me)
    def _():
        pl.semaphore_wait(barrier, 3 + 2 * (N - 1))

    swaps = []
    for i in range(4):
        swaps.append(pltpu.make_async_remote_copy(
            src_ref=t_hbm.at[:, pl.ds(i * W, W)], dst_ref=t.at[:, pl.ds(COLS + i * W, W)],
            send_sem=xs_sem.at[i], recv_sem=xr_sem.at[i], device_id=at(xt, ij, z), device_id_type=MESH))
    swaps.append(pltpu.make_async_remote_copy(
        src_ref=v_hbm, dst_ref=v.at[1], send_sem=xs_sem.at[4], recv_sem=xr_sem.at[4],
        device_id=at(xv, ij, z), device_id_type=MESH))
    for i in (0, 4, 1, 2, 3):
        swaps[i].start()

    def half(q):
        s = q // 4
        return c + s * (1 - 2 * c)

    def to_twin(q):
        pltpu.make_async_remote_copy(
            src_ref=p.at[q, 1 - half(q)], dst_ref=sib.at[q], send_sem=cs_sem, recv_sem=cr_sem.at[q],
            device_id=twin, device_id_type=MESH).start()

    def pair(q):
        res = jnp.dot(v[q // 4], t[:, pl.ds(256 * (q % 4), 256)], preferred_element_type=F32)
        p[q, 0] = res[:, :W]
        p[q, 1] = res[:, W:]
        to_twin(q)

    def single(s, j):
        q = 4 * s + j // 2
        p[q, j % 2] = jnp.dot(v[s], t[:, pl.ds(W * j, W)], preferred_element_type=F32)

        @pl.when(c != (s + j) % 2)
        def _():
            to_twin(q)

    def scatter(q):
        pltpu.make_async_copy(sib.at[q], sib.at[q], cr_sem.at[q]).wait()
        held[q] = p[q, half(q)] + sib[q]
        for d in range(1, N):
            to = (me1 + d) % N
            pltpu.make_async_remote_copy(
                src_ref=held.at[q, pl.ds(pl.multiple_of(to * G, G), G)], dst_ref=s1.at[q, d],
                send_sem=s1s_sem, recv_sem=s1r_sem.at[q], device_id=first(to), device_id_type=MESH).start()

    def gather(q):
        pltpu.make_async_copy(s1.at[q, pl.ds(1, N - 1)], s1.at[q, pl.ds(1, N - 1)], s1r_sem.at[q]).wait()
        total = held[q, pl.ds(pl.multiple_of(me1 * G, G), G), :]
        for d in range(1, N):
            total = total + s1[q, d]
        r1[q] = total
        d = (q - me2 + N) % N

        @pl.when(d == 0)
        def _():
            s2[0] = total

        @pl.when(d != 0)
        def _():
            pltpu.make_async_remote_copy(
                src_ref=r1.at[q], dst_ref=s2.at[d], send_sem=s2s_sem, recv_sem=s2r_sem,
                device_id=second(q), device_id_type=MESH).start()

    load_v.wait()
    load_t.wait()
    pair(0)
    pair(1)
    scatter(0)
    scatter(1)
    swaps[0].wait_recv()
    single(0, 4)
    swaps[1].wait_recv()
    single(0, 5)
    scatter(2)
    swaps[4].wait_recv()
    pair(4)
    pair(5)
    scatter(4)
    single(1, 4)
    single(1, 5)
    scatter(5)
    scatter(6)
    gather(0)
    gather(1)
    gather(2)
    swaps[2].wait_recv()
    single(0, 6)
    single(1, 6)
    scatter(3 + 4 * c)
    gather(4)
    gather(5)
    gather(6)
    gather(3 + 4 * c)
    swaps[3].wait_recv()
    single(0, 7)
    single(1, 7)
    scatter(7 - 4 * c)
    gather(7 - 4 * c)

    pltpu.make_async_copy(s2.at[pl.ds(1, N - 1)], s2.at[pl.ds(1, N - 1)], s2r_sem).wait()
    total = s2[0]
    for d in range(1, N):
        total = total + s2[d]
    fin[...] = total.astype(BF16)

    @pl.when(owner_is_me)
    def _():
        out[...] = fin[...]

    @pl.when(jnp.logical_not(owner_is_me))
    def _():
        last = pltpu.make_async_remote_copy(
            src_ref=fin, dst_ref=out, send_sem=fs_sem, recv_sem=fr_sem,
            device_id=at(owner_x, owner_ij, me1), device_id_type=MESH)
        last.start()
        last.wait()

    for swap in swaps:
        swap.wait_send()
    pltpu.make_async_copy(sib, sib, cs_sem).wait()
    pltpu.make_async_copy(s1.at[:, pl.ds(1, N - 1)], s1.at[:, pl.ds(1, N - 1)], s1s_sem).wait()
    pltpu.make_async_copy(s2.at[pl.ds(1, N - 1)], s2.at[pl.ds(1, N - 1)], s2s_sem).wait()


def per_device(integrals, amplitudes):
    dma, vmem = pltpu.SemaphoreType.DMA, pltpu.VMEM
    return pl.pallas_call(
        kernel,
        out_shape=jax.ShapeDtypeStruct((G, W), BF16),
        in_specs=[pl.BlockSpec(memory_space=pl.ANY)] * 2,
        out_specs=pl.BlockSpec(memory_space=pltpu.VMEM),
        scratch_shapes=[
            vmem((2, ROWS, DEPTH), BF16),
            vmem((DEPTH, 2 * COLS), BF16),
            vmem((N, 2, ROWS, W), F32),
            vmem((N, ROWS, W), F32),
            vmem((N, ROWS, W), F32),
            vmem((N, N, G, W), F32),
            vmem((N, G, W), F32),
            vmem((N, G, W), F32),
            vmem((G, W), BF16),
            dma((2,)), dma((5,)), dma((5,)),
            dma, dma((N,)), dma, dma((N,)), dma, dma, dma, dma,
        ],
        compiler_params=pltpu.CompilerParams(
            collective_id=0, has_side_effects=True, vmem_limit_bytes=48 << 20
        ),
    )(integrals, amplitudes)


def solution(mesh):
    placed = (P("ab", ("cd", "ij")), P(("cd", "ij"), "ab"))
    return jax.shard_map(
        per_device, mesh=mesh, in_specs=placed, out_specs=P(("ab", "cd"), "ij"), check_vma=False
    )
```

time: 197 us -> 71.6 us (0.36)
  the two profiles are of different devices: /device:TPU:6 before, /device:TPU:13 now
where the time goes in v1:
time: 71.6 us; the launch traced here: 71.4 us
  Pallas kernels  68.3 us (95%)
  local copies, waits for them, and re-layouts  3.12 us (4%)
    pallas_call x1, Pallas kernels, per_device(): pl.pallas_call(kernel, out_shape=jax.ShapeDtypeStruct((G, W), BF16), in_s...  68.3 us
    unnamed x5, local copies, waits for them, and re-layouts  3.12 us

profile of v1, /device:TPU:13, one launch (start us, length us, event | category | flops | bytes accessed | tf_op | source)
XLA Modules:
  0.0 71.4 jit_solution(14101180088779432444)
XLA Ops:
  0.0 0.0 copy-start
  0.0 1.3 %copy-done = bf16[1280,512]{1,0:T(8,128)(2,1)S(1)} copy-done((bf16[1280,512]{1,0:T(8,128)(2,1)S(1)}, bf16[1280,512]{1,0:T(8,128)(2,1)}, u32[]{:S(2)}) %copy-start) | copy-done | bytes 1310744
  1.3 0.0 copy-start.1
  1.3 1.2 %copy-done.1 = bf16[384,1280]{1,0:T(8,128)(2,1)S(1)} copy-done((bf16[384,1280]{1,0:T(8,128)(2,1)S(1)}, bf16[384,1280]{1,0:T(8,128)(2,1)}, u32[]{:S(2)}) %copy-start.1) | copy-done | bytes 983064
  2.5 68.3 %shard_map.28 = bf16[48,128]{1,0:T(8,128)(2,1)S(1)} custom-call(bf16[384,1280]{1,0:T(8,128)(2,1)S(1)} %copy-done.1, bf16[1280,512]{1,0:T(8,128)(2,1)S(1)} %copy-done), custom_call_target="tpu_custom_call" | custom-call | tf_op jit(solution)/shard_map/pallas_call | solution.py:207
  70.8 0.6 copy.4
Async XLA Ops:
  0.0 1.3 %copy-start = (bf16[1280,512]{1,0:T(8,128)(2,1)S(1)}, bf16[1280,512]{1,0:T(8,128)(2,1)}, u32[]{:S(2)}) copy-start(bf16[1280,512]{1,0:T(8,128)(2,1)} %t_hbm.1) | copy-start | bytes 3932164
  1.3 1.2 %copy-start.1 = (bf16[384,1280]{1,0:T(8,128)(2,1)S(1)}, bf16[384,1280]{1,0:T(8,128)(2,1)}, u32[]{:S(2)}) copy-start(bf16[384,1280]{1,0:T(8,128)(2,1)} %v_hbm.1) | copy-start | bytes 2949124

commit v2 on v0

v2 whole, which is shorter than its diff:
```python
import jax
import jax.numpy as jnp
from jax import lax
from jax.experimental import pallas as pl
from jax.experimental.pallas import tpu as pltpu
from jax.sharding import PartitionSpec as P

MESH = pl.DeviceIdType.MESH
F32 = jnp.float32
BF16 = jnp.bfloat16
ROWS, DEPTH, COLS = 384, 1280, 512
HALF = 192
LAST = 3
VMEM_BYTES = 62 << 20
N = 8
G = 48
W = 128


def kernel(v_hbm, t_hbm, out, v, t, p, sib, held, s1, r1, s2,
           load_sem, xs_sem, xr_sem, cs_sem, cr_sem, s1s_sem, s1r_sem, s2s_sem, s2r_sem):
    x, ij, z = lax.axis_index("ab"), lax.axis_index("ij"), lax.axis_index("cd")
    y, c = ij // 2, ij % 2
    xv, xt = x + 1 - 2 * (x % 2), 3 - x

    def at(xx, ii, zz):
        return {"ab": xx, "ij": ii, "cd": zz}

    twin = at(x, ij + 1 - 2 * c, z)

    def block(q):
        s = q // 4
        return 2 * (q % 4) + c + s * (1 - 2 * c)

    def over_z(q):
        return 1 if q == LAST else 1 - c

    def peer(zf, i):
        return at(x, 2 * (y + (1 - zf) * (i - y)) + c, z + zf * (i - z))

    def owner(q, zf):
        s, j = q // 4, block(q)
        me1 = y + zf * (z - y)
        return x + s * (xv - x), 4 * (x + (j // 4) * (xt - x)) + j % 4, me1

    def is_me(place):
        return (place[0] == x) & (place[1] == ij) & (place[2] == z)

    slab = ij // 4
    src_s = jnp.where((slab == x) | (slab == 3 - x), 0, 1)
    src_x = x + src_s * (xv - x)
    src_j = jnp.where(slab == src_x, 0, 4) + ij % 4
    src_c = (src_s + src_j) % 2
    src_q = 4 * src_s + src_j // 2
    src_zf = jnp.where((src_c == 0) | (src_q == LAST), 1, 0)

    def source(i):
        return src_x, 2 * (z + src_zf * (i - z)) + src_c, i + src_zf * (z - i)

    barrier = pltpu.get_barrier_semaphore()

    def greet(device):
        pl.semaphore_signal(barrier, inc=1, device_id=device, device_id_type=MESH)

    def greet_other(place):
        @pl.when(jnp.logical_not(is_me(place)))
        def _():
            greet(at(*place))

    greet(at(xt, ij, z))
    greet(at(xv, ij, z))
    greet(twin)

    loads = [pltpu.make_async_copy(v_hbm.at[:, h], v.at[0, h], load_sem.at[h]) for h in range(2)]
    loads.append(pltpu.make_async_copy(t_hbm, t.at[:, pl.ds(0, COLS)], load_sem.at[2]))
    for load in loads:
        load.start()

    for d in range(1, N):
        greet(peer(1, (z + d) % N))

    @pl.when(c == 1)
    def _():
        for d in range(1, N):
            greet(peer(0, (y + d) % N))

    for q in range(N):
        greet_other(owner(q, over_z(q)))
    for i in range(N):
        greet_other(source(i))

    mine = jnp.where(is_me(source(y + (1 - src_zf) * (z - y))), 1, 0)

    def settle(count):
        pl.semaphore_wait(barrier, count)

    for cc in range(2):
        for m in range(2):
            @pl.when((c == cc) & (mine == m))
            def _():
                settle(3 + 7 + 7 * cc + 16 - 2 * m)

    swaps = []
    for i in range(4):
        swaps.append(pltpu.make_async_remote_copy(
            src_ref=t_hbm.at[:, pl.ds(i * W, W)], dst_ref=t.at[:, pl.ds(COLS + i * W, W)],
            send_sem=xs_sem.at[i], recv_sem=xr_sem.at[i], device_id=at(xt, ij, z), device_id_type=MESH))
    for h in range(2):
        swaps.append(pltpu.make_async_remote_copy(
            src_ref=v_hbm.at[:, h], dst_ref=v.at[1, h], send_sem=xs_sem.at[4 + h], recv_sem=xr_sem.at[4 + h],
            device_id=at(xv, ij, z), device_id_type=MESH))
    for i in (0, 4, 1, 5, 2, 3):
        swaps[i].start()

    def to_twin(q, h):
        mine_b = block(q) % 2
        pltpu.make_async_remote_copy(
            src_ref=p.at[q, 1 - mine_b, h], dst_ref=sib.at[q, h], send_sem=cs_sem, recv_sem=cr_sem.at[q, h],
            device_id=twin, device_id_type=MESH).start()

    def pair(q, h):
        rows = v[q // 4, h].reshape(HALF, DEPTH)
        res = jnp.dot(rows, t[:, pl.ds(256 * (q % 4), 256)], preferred_element_type=F32)
        p[q, 0, h] = res[:, :W]
        p[q, 1, h] = res[:, W:]
        to_twin(q, h)

    def single(s, h, j):
        q = 4 * s + j // 2
        rows = v[s, h].reshape(HALF, DEPTH)
        p[q, j % 2, h] = jnp.dot(rows, t[:, pl.ds(W * j, W)], preferred_element_type=F32)

        @pl.when(c != (s + j) % 2)
        def _():
            to_twin(q, h)

    def scatter(q, h, zf):
        pltpu.make_async_copy(sib.at[q, h], sib.at[q, h], cr_sem.at[q, h]).wait()
        held[q, h] = p[q, block(q) % 2, h] + sib[q, h]
        me1 = y + zf * (z - y)
        for i in range(4):
            g = 2 * i + h

            @pl.when(g != me1)
            def _():
                pltpu.make_async_remote_copy(
                    src_ref=held.at[q, h, pl.ds(G * i, G)], dst_ref=s1.at[q, (g - me1 + N) % N],
                    send_sem=s1s_sem, recv_sem=s1r_sem.at[q], device_id=peer(zf, g), device_id_type=MESH).start()

    def gather(q, zf):
        pltpu.make_async_copy(s1.at[q, pl.ds(1, N - 1)], s1.at[q, pl.ds(1, N - 1)], s1r_sem.at[q]).wait()
        me1 = y + zf * (z - y)
        me2 = z + zf * (y - z)
        total = held[q, me1 % 2, pl.ds(pl.multiple_of(me1 // 2 * G, G), G), :]
        for d in range(1, N):
            total = total + s1[q, d]
        place = owner(q, zf)
        here = is_me(place)

        @pl.when(here)
        def _():
            s2[me2] = total
            r1[q] = total

        @pl.when(jnp.logical_not(here))
        def _():
            r1[q] = total
            pltpu.make_async_remote_copy(
                src_ref=r1.at[q], dst_ref=s2.at[me2], send_sem=s2s_sem, recv_sem=s2r_sem,
                device_id=at(*place), device_id_type=MESH).start()

    for load in loads:
        load.wait()
    for q in (0, 1):
        for h in (0, 1):
            pair(q, h)
    for q in (0, 1):
        for h in (0, 1):
            scatter(q, h, 1 - c)
    swaps[0].wait_recv()
    single(0, 0, 4)
    single(0, 1, 4)
    swaps[4].wait_recv()
    pair(4, 0)
    pair(5, 0)
    single(1, 0, 4)
    gather(0, 1 - c)
    gather(1, 1 - c)
    scatter(4, 0, 1 - c)
    scatter(5, 0, 1 - c)
    swaps[1].wait_recv()
    single(0, 0, 5)
    single(0, 1, 5)
    single(1, 0, 5)
    scatter(2, 0, 1 - c)
    scatter(2, 1, 1 - c)
    scatter(6, 0, 1 - c)
    swaps[5].wait_recv()
    pair(4, 1)
    pair(5, 1)
    single(1, 1, 4)
    single(1, 1, 5)
    scatter(4, 1, 1 - c)
    scatter(5, 1, 1 - c)
    scatter(6, 1, 1 - c)
    swaps[2].wait_recv()
    single(0, 0, 6)
    single(0, 1, 6)
    single(1, 0, 6)
    single(1, 1, 6)
    for cc in range(2):
        @pl.when(c == cc)
        def _():
            scatter(3 + 4 * cc, 0, 1 - cc)
            scatter(3 + 4 * cc, 1, 1 - cc)
    gather(2, 1 - c)
    swaps[3].wait_recv()
    single(0, 0, 7)
    single(0, 1, 7)
    single(1, 0, 7)
    single(1, 1, 7)
    for cc in range(2):
        @pl.when(c == cc)
        def _():
            scatter(7 - 4 * cc, 0, 1)
            scatter(7 - 4 * cc, 1, 1)
    gather(4, 1 - c)
    gather(5, 1 - c)
    gather(6, 1 - c)
    for cc in range(2):
        @pl.when(c == cc)
        def _():
            gather(3 + 4 * cc, 1 - cc)
            gather(7 - 4 * cc, 1)

    for m in range(2):
        @pl.when(mine == m)
        def _():
            pltpu.make_async_copy(s2.at[pl.ds(0, N - m)], s2.at[pl.ds(0, N - m)], s2r_sem).wait()
    total = s2[0]
    for d in range(1, N):
        total = total + s2[d]
    out[...] = total.astype(BF16)

    for swap in swaps:
        swap.wait_send()
    pltpu.make_async_copy(sib, sib, cs_sem).wait()
    pltpu.make_async_copy(s1.at[:, pl.ds(1, N - 1)], s1.at[:, pl.ds(1, N - 1)], s1s_sem).wait()
    for m in range(2):
        @pl.when(mine == m)
        def _():
            pltpu.make_async_copy(s2.at[pl.ds(0, N - m)], s2.at[pl.ds(0, N - m)], s2s_sem).wait()


def per_device(integrals, amplitudes):
    dma, vmem = pltpu.SemaphoreType.DMA, pltpu.VMEM
    return pl.pallas_call(
        kernel,
        out_shape=jax.ShapeDtypeStruct((G, W), BF16),
        in_specs=[pl.BlockSpec(memory_space=pl.ANY)] * 2,
        out_specs=pl.BlockSpec(memory_space=pltpu.VMEM),
        scratch_shapes=[
            vmem((2, 2, 4, G, DEPTH), BF16),
            vmem((DEPTH, 2 * COLS), BF16),
            vmem((N, 2, 2, HALF, W), F32),
            vmem((N, 2, HALF, W), F32),
            vmem((N, 2, HALF, W), F32),
            vmem((N, N, G, W), F32),
            vmem((N, G, W), F32),
            vmem((N, G, W), F32),
            dma((3,)), dma((6,)), dma((6,)),
            dma, dma((N, 2)), dma, dma((N,)), dma, dma,
        ],
        compiler_params=pltpu.CompilerParams(
            collective_id=0, has_side_effects=True, vmem_limit_bytes=VMEM_BYTES
        ),
    )(integrals.reshape(4, 2, G, DEPTH), amplitudes)


def solution(mesh):
    placed = (P("ab", ("cd", "ij")), P(("cd", "ij"), "ab"))
    return jax.shard_map(
        per_device, mesh=mesh, in_specs=placed, out_specs=P(("ab", "cd"), "ij"), check_vma=False
    )
```

time: 197 us -> 61.8 us (0.31)
  the two profiles are of different devices: /device:TPU:6 before, /device:TPU:13 now
where the time goes in v2:
time: 61.8 us; the launch traced here: 61.6 us
  Pallas kernels  60.3 us (98%)
  local copies, waits for them, and re-layouts  1.31 us (2%)
    pallas_call x1, Pallas kernels, per_device(): pl.pallas_call(kernel, out_shape=jax.ShapeDtypeStruct((G, W), BF16), in_s...  60.3 us
    unnamed x1, local copies, waits for them, and re-layouts  1.31 us

profile of v2, /device:TPU:13, one launch (start us, length us, event | category | flops | bytes accessed | tf_op | source)
XLA Modules:
  0.0 61.6 jit_solution(4353050242134259749)
XLA Ops:
  0.0 60.3 %shard_map.28 = bf16[48,128]{1,0:T(8,128)(2,1)} custom-call(bf16[4,2,48,1280]{3,2,1,0:T(8,128)(2,1)} %bitcast.1, bf16[1280,512]{1,0:T(8,128)(2,1)} %t_hbm.1), custom_call_target="tpu_custom_call" | custom-call | tf_op jit(solution)/shard_map/pallas_call | solution.py:257
  60.3 1.3 %copy.4 = bf16[48,128]{1,0:T(8,128)(2,1)} copy(bf16[48,128]{1,0:T(8,128)(2,1)} %shard_map.28) | data formatting | bytes 24576

commit v3 on v2

--- a/solution.py
+++ b/solution.py
@@ -10,7 +10,6 @@
 BF16 = jnp.bfloat16
 ROWS, DEPTH, COLS = 384, 1280, 512
 HALF = 192
-LAST = 3
 VMEM_BYTES = 62 << 20
 N = 8
 G = 48
@@ -18,7 +17,7 @@
 
 
 def kernel(v_hbm, t_hbm, out, v, t, p, sib, held, s1, r1, s2,
-           load_sem, xs_sem, xr_sem, cs_sem, cr_sem, s1s_sem, s1r_sem, s2s_sem, s2r_sem):
+           load_sem, xs_sem, xr_sem, cs_sem, cr_sem, s1s_sem, s1r_sem, s2s_sem, s2r_sem, line_sem, wide_sem):
     x, ij, z = lax.axis_index("ab"), lax.axis_index("ij"), lax.axis_index("cd")
     y, c = ij // 2, ij % 2
     xv, xt = x + 1 - 2 * (x % 2), 3 - x
@@ -28,77 +27,47 @@
 
     twin = at(x, ij + 1 - 2 * c, z)
 
+    me1 = z + c * (y - z)
+    me2 = y + c * (z - y)
+
     def block(q):
         s = q // 4
         return 2 * (q % 4) + c + s * (1 - 2 * c)
 
-    def over_z(q):
-        return 1 if q == LAST else 1 - c
-
-    def peer(zf, i):
-        return at(x, 2 * (y + (1 - zf) * (i - y)) + c, z + zf * (i - z))
-
-    def owner(q, zf):
+    def peer(i):
+        return at(x, 2 * (y + c * (i - y)) + c, z + (1 - c) * (i - z))
+
+    def owner(q):
         s, j = q // 4, block(q)
-        me1 = y + zf * (z - y)
         return x + s * (xv - x), 4 * (x + (j // 4) * (xt - x)) + j % 4, me1
 
     def is_me(place):
         return (place[0] == x) & (place[1] == ij) & (place[2] == z)
 
     slab = ij // 4
-    src_s = jnp.where((slab == x) | (slab == 3 - x), 0, 1)
-    src_x = x + src_s * (xv - x)
-    src_j = jnp.where(slab == src_x, 0, 4) + ij % 4
-    src_c = (src_s + src_j) % 2
-    src_q = 4 * src_s + src_j // 2
-    src_zf = jnp.where((src_c == 0) | (src_q == LAST), 1, 0)
-
-    def source(i):
-        return src_x, 2 * (z + src_zf * (i - z)) + src_c, i + src_zf * (z - i)
+    own_s = (slab == x) | (slab == 3 - x)
+    mine = jnp.where(own_s & ((c == 0) | (y == z)), 1, 0)
 
     barrier = pltpu.get_barrier_semaphore()
 
-    def greet(device):
-        pl.semaphore_signal(barrier, inc=1, device_id=device, device_id_type=MESH)
-
-    def greet_other(place):
-        @pl.when(jnp.logical_not(is_me(place)))
-        def _():
-            greet(at(*place))
-
-    greet(at(xt, ij, z))
-    greet(at(xv, ij, z))
-    greet(twin)
+    def signal(sem, device):
+        pl.semaphore_signal(sem, inc=1, device_id=device, device_id_type=MESH)
+
+    signal(barrier, at(xt, 2 * y, z))
+    signal(barrier, at(xv, 2 * y, z))
 
     loads = [pltpu.make_async_copy(v_hbm.at[:, h], v.at[0, h], load_sem.at[h]) for h in range(2)]
     loads.append(pltpu.make_async_copy(t_hbm, t.at[:, pl.ds(0, COLS)], load_sem.at[2]))
-    for load in loads:
-        load.start()
-
-    for d in range(1, N):
-        greet(peer(1, (z + d) % N))
+
+    @pl.when(c == 0)
+    def _():
+        pl.semaphore_wait(barrier, 5)
+        signal(line_sem, twin)
 
     @pl.when(c == 1)
     def _():
-        for d in range(1, N):
-            greet(peer(0, (y + d) % N))
-
-    for q in range(N):
-        greet_other(owner(q, over_z(q)))
-    for i in range(N):
-        greet_other(source(i))
-
-    mine = jnp.where(is_me(source(y + (1 - src_zf) * (z - y))), 1, 0)
-
-    def settle(count):
-        pl.semaphore_wait(barrier, count)
-
-    for cc in range(2):
-        for m in range(2):
-            @pl.when((c == cc) & (mine == m))
-            def _():
-                settle(3 + 7 + 7 * cc + 16 - 2 * m)
+        signal(barrier, twin)
+        pl.semaphore_wait(line_sem, 1)
 
     swaps = []
     for i in range(4):
@@ -112,6 +81,15 @@
     for i in (0, 4, 1, 5, 2, 3):
         swaps[i].start()
 
+    for load in loads:
+        load.start()
+
+    @pl.when(c == 1)
+    def _():
+        for d in range(1, N):
+            signal(barrier, at(x, ij, (z + d) % N))
+            signal(barrier, at(x, 2 * ((y + d) % N) + 1, z))
+
     def to_twin(q, h):
         mine_b = block(q) % 2
         pltpu.make_async_remote_copy(
@@ -134,10 +112,9 @@
         def _():
             to_twin(q, h)
 
-    def scatter(q, h, zf):
+    def scatter(q, h):
         pltpu.make_async_copy(sib.at[q, h], sib.at[q, h], cr_sem.at[q, h]).wait()
         held[q, h] = p[q, block(q) % 2, h] + sib[q, h]
-        me1 = y + zf * (z - y)
         for i in range(4):
             g = 2 * i + h
 
@@ -145,16 +122,14 @@
             def _():
                 pltpu.make_async_remote_copy(
                     src_ref=held.at[q, h, pl.ds(G * i, G)], dst_ref=s1.at[q, (g - me1 + N) % N],
-                    send_sem=s1s_sem, recv_sem=s1r_sem.at[q], device_id=peer(zf, g), device_id_type=MESH).start()
-
-    def gather(q, zf):
+                    send_sem=s1s_sem, recv_sem=s1r_sem.at[q], device_id=peer(g), device_id_type=MESH).start()
+
+    def gather(q):
         pltpu.make_async_copy(s1.at[q, pl.ds(1, N - 1)], s1.at[q, pl.ds(1, N - 1)], s1r_sem.at[q]).wait()
-        me1 = y + zf * (z - y)
-        me2 = z + zf * (y - z)
         total = held[q, me1 % 2, pl.ds(pl.multiple_of(me1 // 2 * G, G), G), :]
         for d in range(1, N):
             total = total + s1[q, d]
-        place = owner(q, zf)
+        place = owner(q)
         here = is_me(place)
 
         @pl.when(here)
@@ -174,9 +149,19 @@
     for q in (0, 1):
         for h in (0, 1):
             pair(q, h)
+
+    @pl.when(c == 1)
+    def _():
+        pl.semaphore_wait(barrier, 2 * (N - 1))
+        signal(wide_sem, twin)
+
+    @pl.when(c == 0)
+    def _():
+        pl.semaphore_wait(wide_sem, 1)
+
     for q in (0, 1):
         for h in (0, 1):
-            scatter(q, h, 1 - c)
+            scatter(q, h)
     swaps[0].wait_recv()
     single(0, 0, 4)
     single(0, 1, 4)
@@ -184,25 +169,25 @@
     pair(4, 0)
     pair(5, 0)
     single(1, 0, 4)
-    gather(0, 1 - c)
-    gather(1, 1 - c)
-    scatter(4, 0, 1 - c)
-    scatter(5, 0, 1 - c)
+    gather(0)
+    gather(1)
+    scatter(4, 0)
+    scatter(5, 0)
     swaps[1].wait_recv()
     single(0, 0, 5)
     single(0, 1, 5)
     single(1, 0, 5)
-    scatter(2, 0, 1 - c)
-    scatter(2, 1, 1 - c)
-    scatter(6, 0, 1 - c)
+    scatter(2, 0)
+    scatter(2, 1)
+    scatter(6, 0)
     swaps[5].wait_recv()
     pair(4, 1)
     pair(5, 1)
     single(1, 1, 4)
     single(1, 1, 5)
-    scatter(4, 1, 1 - c)
-    scatter(5, 1, 1 - c)
-    scatter(6, 1, 1 - c)
+    scatter(4, 1)
+    scatter(5, 1)
+    scatter(6, 1)
     swaps[2].wait_recv()
     single(0, 0, 6)
     single(0, 1, 6)
@@ -211,9 +196,9 @@
     for cc in range(2):
         @pl.when(c == cc)
         def _():
-            scatter(3 + 4 * cc, 0, 1 - cc)
-            scatter(3 + 4 * cc, 1, 1 - cc)
-    gather(2, 1 - c)
+            scatter(3 + 4 * cc, 0)
+            scatter(3 + 4 * cc, 1)
+    gather(2)
     swaps[3].wait_recv()
     single(0, 0, 7)
     single(0, 1, 7)
@@ -222,16 +207,16 @@
     for cc in range(2):
         @pl.when(c == cc)
         def _():
-            scatter(7 - 4 * cc, 0, 1)
-            scatter(7 - 4 * cc, 1, 1)
-    gather(4, 1 - c)
-    gather(5, 1 - c)
-    gather(6, 1 - c)
+            scatter(7 - 4 * cc, 0)
+            scatter(7 - 4 * cc, 1)
+    gather(4)
+    gather(5)
+    gather(6)
     for cc in range(2):
         @pl.when(c == cc)
         def _():
-            gather(3 + 4 * cc, 1 - cc)
-            gather(7 - 4 * cc, 1)
+            gather(3 + 4 * cc)
+            gather(7 - 4 * cc)
 
     for m in range(2):
         @pl.when(mine == m)
@@ -270,6 +255,7 @@
             vmem((N, G, W), F32),
             dma((3,)), dma((6,)), dma((6,)),
             dma, dma((N, 2)), dma, dma((N,)), dma, dma,
+            pltpu.SemaphoreType.REGULAR, pltpu.SemaphoreType.REGULAR,
         ],
         compiler_params=pltpu.CompilerParams(
             collective_id=0, has_side_effects=True, vmem_limit_bytes=VMEM_BYTES

time: 61.8 us -> 58 us (0.939)
  the two profiles are of different devices: /device:TPU:13 before, /device:TPU:77 now
where the time goes in v3:
time: 58 us; the launch traced here: 57.8 us
  Pallas kernels  56.5 us (97%)
  local copies, waits for them, and re-layouts  1.31 us (2%)
    pallas_call x1, Pallas kernels, per_device(): pl.pallas_call(kernel, out_shape=jax.ShapeDtypeStruct((G, W), BF16), in_s...  56.5 us
    unnamed x1, local copies, waits for them, and re-layouts  1.31 us

profile of v3, /device:TPU:77, one launch (start us, length us, event | category | flops | bytes accessed | tf_op | source)
XLA Modules:
  0.0 57.8 jit_solution(7831038617766586587)
XLA Ops:
  0.0 56.5 %shard_map.28 = bf16[48,128]{1,0:T(8,128)(2,1)} custom-call(bf16[4,2,48,1280]{3,2,1,0:T(8,128)(2,1)} %bitcast.1, bf16[1280,512]{1,0:T(8,128)(2,1)} %t_hbm.1), custom_call_target="tpu_custom_call" | custom-call | tf_op jit(solution)/shard_map/pallas_call | solution.py:242
  56.5 1.3 %copy.4 = bf16[48,128]{1,0:T(8,128)(2,1)} copy(bf16[48,128]{1,0:T(8,128)(2,1)} %shard_map.28) | data formatting | bytes 24576

commit v4 on v3

v4 whole, which is shorter than its diff:
```python
import jax
import jax.numpy as jnp
from jax import lax
from jax.experimental import pallas as pl
from jax.experimental.pallas import tpu as pltpu
from jax.sharding import PartitionSpec as P

MESH = pl.DeviceIdType.MESH
F32 = jnp.float32
BF16 = jnp.bfloat16
ROWS, DEPTH, COLS = 384, 1280, 512
PART = 96
VMEM_BYTES = 53 << 20
N = 8
G = 48
W = 128
Z_FIRST = (5,)
ALL = (0, 4)


def kernel(v_hbm, t_hbm, out, v, t, p, sib, held, s1, r1, s2,
           load_sem, xs_sem, xr_sem, cs_sem, cr_sem, s1s_sem, s1r_sem, s2s_sem, s2r_sem, line_sem, wide_sem):
    x, ij, z = lax.axis_index("ab"), lax.axis_index("ij"), lax.axis_index("cd")
    y, c = ij // 2, ij % 2
    xv, xt = x + 1 - 2 * (x % 2), 3 - x

    def at(xx, ii, zz):
        return {"ab": xx, "ij": ii, "cd": zz}

    twin = at(x, ij + 1 - 2 * c, z)

    def axes(q):
        yf = c * (0 if isinstance(q, int) and q in Z_FIRST else 1)
        return yf, z + yf * (y - z), y + yf * (z - y)

    def block(q):
        s = q // 4
        return 2 * (q % 4) + c + s * (1 - 2 * c)

    def peer(yf, i):
        return at(x, 2 * (y + yf * (i - y)) + c, z + (1 - yf) * (i - z))

    def owner(q):
        s, j = q // 4, block(q)
        return x + s * (xv - x), 4 * (x + (j // 4) * (xt - x)) + j % 4, axes(q)[1]

    def is_me(place):
        return (place[0] == x) & (place[1] == ij) & (place[2] == z)

    slab = ij // 4
    own_s = (slab == x) | (slab == 3 - x)
    mine = jnp.where(own_s & ((c == 0) | (y == z)), 1, 0)

    barrier = pltpu.get_barrier_semaphore()

    def signal(sem, device):
        pl.semaphore_signal(sem, inc=1, device_id=device, device_id_type=MESH)

    signal(barrier, at(xt, 2 * y, z))
    signal(barrier, at(xv, 2 * y, z))

    loads = [pltpu.make_async_copy(v_hbm.at[:, h], v.at[0, h], load_sem.at[h]) for h in range(4)]
    loads.append(pltpu.make_async_copy(t_hbm, t.at[:, pl.ds(0, COLS)], load_sem.at[4]))

    @pl.when(c == 0)
    def _():
        pl.semaphore_wait(barrier, 5)
        signal(line_sem, twin)

    @pl.when(c == 1)
    def _():
        signal(barrier, twin)
        pl.semaphore_wait(line_sem, 1)

    def remote(src, dst, send, recv, device):
        return pltpu.make_async_remote_copy(
            src_ref=src, dst_ref=dst, send_sem=send, recv_sem=recv, device_id=device, device_id_type=MESH)

    over_t, over_v = at(xt, ij, z), at(xv, ij, z)
    swaps = [remote(t_hbm.at[:, pl.ds(i * W, W)], t.at[:, pl.ds(COLS + i * W, W)], xs_sem.at[i], xr_sem.at[i], over_t)
             for i in range(4)]
    swaps += [remote(v_hbm.at[:, h], v.at[1, h], xs_sem.at[4 + h], xr_sem.at[4 + h], over_v) for h in range(4)]
    for i in (0, 4, 1, 5, 2, 6, 3, 7):
        swaps[i].start()

    for load in loads:
        load.start()

    @pl.when(c == 1)
    def _():
        for d in range(1, N):
            signal(barrier, at(x, ij, (z + d) % N))
            signal(barrier, at(x, 2 * ((y + d) % N) + 1, z))

    def to_twin(src, dst, sem):
        remote(src, dst, cs_sem, sem, twin).start()

    def pair(s, jj, parts):
        q = 4 * s + jj
        lo, n = parts
        rows = v[s, pl.ds(lo, n)].reshape(n * PART, DEPTH)
        res = jnp.dot(rows, t[:, pl.ds(2 * W * jj, 2 * W)], preferred_element_type=F32)
        for b in range(2):
            p[q, b, pl.ds(lo, n)] = res[:, b * W:(b + 1) * W].reshape(n, PART, W)
        other = 1 - block(q) % 2
        to_twin(p.at[q, other, pl.ds(lo, n)], sib.at[q, pl.ds(lo, n)], cr_sem.at[q, lo])

    def single(s, j, parts):
        q = 4 * s + j // 2
        lo, n = parts
        rows = v[s, pl.ds(lo, n)].reshape(n * PART, DEPTH)
        res = jnp.dot(rows, t[:, pl.ds(W * j, W)], preferred_element_type=F32)
        p[q, j % 2, pl.ds(lo, n)] = res.reshape(n, PART, W)

        @pl.when(c != (s + j) % 2)
        def _():
            to_twin(p.at[q, j % 2, pl.ds(lo, n)], sib.at[q, pl.ds(lo, n)], cr_sem.at[q, lo])

    def add_twin(q, parts):
        lo, n = parts
        piece = sib.at[q, pl.ds(lo, n)]
        pltpu.make_async_copy(piece, piece, cr_sem.at[q, lo]).wait()
        held[q, pl.ds(lo, n)] = p[q, block(q) % 2, pl.ds(lo, n)] + sib[q, pl.ds(lo, n)]

    def to_peer(q, h, i, slot):
        remote(held.at[q, h, pl.ds(pl.multiple_of(G * i, G), G)], s1.at[q, slot], s1s_sem, s1r_sem.at[q], peer(axes(q)[0], h + 4 * i)).start()

    def scatter(q):
        add_twin(q, ALL)
        me1 = axes(q)[1]
        for d in range(1, N):
            to = (me1 + d) % N
            to_peer(q, to % 4, to // 4, d)

    def scatter_part(q, h):
        add_twin(q, (h, 1))
        me1 = axes(q)[1]
        for i in range(2):
            g = h + 4 * i

            @pl.when(g != me1)
            def _():
                to_peer(q, h, i, (g - me1 + N) % N)

    def gather(q):
        pltpu.make_async_copy(s1.at[q, pl.ds(1, N - 1)], s1.at[q, pl.ds(1, N - 1)], s1r_sem.at[q]).wait()
        yf, me1, me2 = axes(q)
        total = held[q, me1 % 4, pl.ds(pl.multiple_of(me1 // 4 * G, G), G), :]
        for d in range(1, N):
            total = total + s1[q, d]
        place = owner(q)
        here = is_me(place)

        @pl.when(here)
        def _():
            s2[me2] = total
            r1[q] = total

        @pl.when(jnp.logical_not(here))
        def _():
            r1[q] = total
            pltpu.make_async_remote_copy(
                src_ref=r1.at[q], dst_ref=s2.at[me2], send_sem=s2s_sem, recv_sem=s2r_sem,
                device_id=at(*place), device_id_type=MESH).start()

    for load in loads:
        load.wait()
    pair(0, 0, ALL)
    pair(0, 1, ALL)

    @pl.when(c == 1)
    def _():
        pl.semaphore_wait(barrier, 2 * (N - 1))
        signal(wide_sem, twin)

    @pl.when(c == 0)
    def _():
        pl.semaphore_wait(wide_sem, 1)

    scatter(0)
    scatter(1)
    swaps[4].wait_recv()
    pair(1, 0, (0, 1))
    pair(1, 1, (0, 1))
    scatter_part(4, 0)
    scatter_part(5, 0)
    swaps[0].wait_recv()
    single(0, 4, ALL)
    swaps[5].wait_recv()
    pair(1, 0, (1, 1))
    pair(1, 1, (1, 1))
    single(1, 4, (0, 1))
    single(1, 4, (1, 1))
    scatter_part(4, 1)
    scatter_part(5, 1)
    swaps[1].wait_recv()
    single(0, 5, ALL)
    single(1, 5, (0, 1))
    single(1, 5, (1, 1))
    scatter(2)
    scatter_part(6, 0)
    scatter_part(6, 1)

    gather(0)
    gather(1)
    for h in (2, 3):
        swaps[4 + h].wait_recv()
        pair(1, 0, (h, 1))
        pair(1, 1, (h, 1))
        single(1, 4, (h, 1))
        single(1, 5, (h, 1))
        for q in (4, 5, 6):
            scatter_part(q, h)
    swaps[2].wait_recv()
    single(0, 6, ALL)
    single(1, 6, ALL)
    scatter(3 + 4 * c)
    gather(2)
    swaps[3].wait_recv()
    for cc in range(2):
        @pl.when(c == cc)
        def _():
            for lo in (0, 2):
                for s in (cc, 1 - cc):
                    single(s, 7, (lo, 2))

    def send_last(*groups):
        me1 = axes(7 - 4 * c)[1]
        for g in groups:
            @pl.when(g != me1)
            def _():
                to_peer(7 - 4 * c, g % 4, g // 4, (g - me1 + N) % N)

    add_twin(7 - 4 * c, (0, 2))
    send_last(0, 1)
    add_twin(7 - 4 * c, (2, 2))
    send_last(2, 3, 4, 5, 6, 7)
    gather(4)
    gather(5)
    gather(6)
    gather(3 + 4 * c)
    gather(7 - 4 * c)

    for m in range(2):
        @pl.when(mine == m)
        def _():
            pltpu.make_async_copy(s2.at[pl.ds(0, N - m)], s2.at[pl.ds(0, N - m)], s2r_sem).wait()
    total = s2[0]
    for d in range(1, N):
        total = total + s2[d]
    out[...] = total.astype(BF16)

    for swap in swaps:
        swap.wait_send()

    pltpu.make_async_copy(sib, sib, cs_sem).wait()
    pltpu.make_async_copy(s1.at[:, pl.ds(1, N - 1)], s1.at[:, pl.ds(1, N - 1)], s1s_sem).wait()
    for m in range(2):
        @pl.when(mine == m)
        def _():
            pltpu.make_async_copy(s2.at[pl.ds(0, N - m)], s2.at[pl.ds(0, N - m)], s2s_sem).wait()


def per_device(integrals, amplitudes):
    dma, vmem = pltpu.SemaphoreType.DMA, pltpu.VMEM
    return pl.pallas_call(
        kernel,
        out_shape=jax.ShapeDtypeStruct((G, W), BF16),
        in_specs=[pl.BlockSpec(memory_space=pl.ANY)] * 2,
        out_specs=pl.BlockSpec(memory_space=pltpu.VMEM),
        scratch_shapes=[
            vmem((2, 4, 2, G, DEPTH), BF16),
            vmem((DEPTH, 2 * COLS), BF16),
            vmem((N, 2, 4, PART, W), F32),
            vmem((N, 4, PART, W), F32),
            vmem((N, 4, PART, W), F32),
            vmem((N, N, G, W), F32),
            vmem((N, G, W), F32),
            vmem((N, G, W), F32),
            dma((5,)), dma((8,)), dma((8,)),
            dma, dma((N, 4)), dma, dma((N,)), dma, dma,
            pltpu.SemaphoreType.REGULAR, pltpu.SemaphoreType.REGULAR,
        ],
        compiler_params=pltpu.CompilerParams(
            collective_id=0, has_side_effects=True, vmem_limit_bytes=VMEM_BYTES
        ),
    )(integrals.reshape(2, 4, G, DEPTH), amplitudes)


def solution(mesh):
    placed = (P("ab", ("cd", "ij")), P(("cd", "ij"), "ab"))
    return jax.shard_map(
        per_device, mesh=mesh, in_specs=placed, out_specs=P(("ab", "cd"), "ij"), check_vma=False
    )
```

time: 58 us -> 56 us (0.966)
  the two profiles are of different devices: /device:TPU:77 before, /device:TPU:13 now
where the time goes in v4:
time: 56 us; the launch traced here: 55.9 us
  Pallas kernels  55.3 us (99%)
  local copies, waits for them, and re-layouts  0.6 us (1%)
    pallas_call x1, Pallas kernels, per_device(): pl.pallas_call(kernel, out_shape=jax.ShapeDtypeStruct((G, W), BF16), in_s...  55.3 us

profile of v4, /device:TPU:13, one launch (start us, length us, event | category | flops | bytes accessed | tf_op | source)
XLA Modules:
  0.0 55.9 jit_solution(140320188220140648)
XLA Ops:
  0.0 55.3 %shard_map.28 = bf16[48,128]{1,0:T(8,128)(2,1)S(1)} custom-call(bf16[2,4,48,1280]{3,2,1,0:T(8,128)(2,1)} %bitcast.1, bf16[1280,512]{1,0:T(8,128)(2,1)} %t_hbm.1), custom_call_target="tpu_custom_call" | custom-call | tf_op jit(solution)/shard_map/pallas_call | solution.py:266
  55.3 0.6 %copy.4 = bf16[48,128]{1,0:T(8,128)(2,1)} copy(bf16[48,128]{1,0:T(8,128)(2,1)S(1)} %shard_map.28) | data formatting | bytes 24576

commit v5 on v4

--- a/solution.py
+++ b/solution.py
@@ -22,7 +22,7 @@
            load_sem, xs_sem, xr_sem, cs_sem, cr_sem, s1s_sem, s1r_sem, s2s_sem, s2r_sem, line_sem, wide_sem):
     x, ij, z = lax.axis_index("ab"), lax.axis_index("ij"), lax.axis_index("cd")
     y, c = ij // 2, ij % 2
-    xv, xt = x + 1 - 2 * (x % 2), 3 - x
+    xv, xt = 3 - x, x + 1 - 2 * (x % 2)
 
     def at(xx, ii, zz):
         return {"ab": xx, "ij": ii, "cd": zz}
@@ -48,7 +48,7 @@
         return (place[0] == x) & (place[1] == ij) & (place[2] == z)
 
     slab = ij // 4
-    own_s = (slab == x) | (slab == 3 - x)
+    own_s = (slab == x) | (slab == xt)
     mine = jnp.where(own_s & ((c == 0) | (y == z)), 1, 0)
 
     barrier = pltpu.get_barrier_semaphore()
@@ -61,6 +61,8 @@
 
     loads = [pltpu.make_async_copy(v_hbm.at[:, h], v.at[0, h], load_sem.at[h]) for h in range(4)]
     loads.append(pltpu.make_async_copy(t_hbm, t.at[:, pl.ds(0, COLS)], load_sem.at[4]))
+    for load in loads:
+        load.start()
 
     @pl.when(c == 0)
     def _():
@@ -82,9 +84,6 @@
     swaps += [remote(v_hbm.at[:, h], v.at[1, h], xs_sem.at[4 + h], xr_sem.at[4 + h], over_v) for h in range(4)]
     for i in (0, 4, 1, 5, 2, 6, 3, 7):
         swaps[i].start()
-
-    for load in loads:
-        load.start()
 
     @pl.when(c == 1)
     def _():

time: 56 us -> 55.9 us (level)
  the two profiles are of different devices: /device:TPU:13 before, /device:TPU:203 now
where the time goes in v5:
time: 55.9 us; the launch traced here: 55.7 us
  Pallas kernels  55.1 us (99%)
  local copies, waits for them, and re-layouts  0.6 us (1%)
    pallas_call x1, Pallas kernels, per_device(): pl.pallas_call(kernel, out_shape=jax.ShapeDtypeStruct((G, W), BF16), in_s...  55.1 us

profile of v5, /device:TPU:203, one launch (start us, length us, event | category | flops | bytes accessed | tf_op | source)
XLA Modules:
  0.0 55.7 jit_solution(17294958637058484246)
XLA Ops:
  0.0 55.1 %shard_map.28 = bf16[48,128]{1,0:T(8,128)(2,1)S(1)} custom-call(bf16[2,4,48,1280]{3,2,1,0:T(8,128)(2,1)} %bitcast.1, bf16[1280,512]{1,0:T(8,128)(2,1)} %t_hbm.1), custom_call_target="tpu_custom_call" | custom-call | tf_op jit(solution)/shard_map/pallas_call | solution.py:265
  55.1 0.6 %copy.4 = bf16[48,128]{1,0:T(8,128)(2,1)} copy(bf16[48,128]{1,0:T(8,128)(2,1)S(1)} %shard_map.28) | data formatting | bytes 24576

commit v6 on v5

--- a/solution.py
+++ b/solution.py
@@ -233,7 +233,7 @@
     add_twin(7 - 4 * c, (0, 2))
     send_last(0, 1)
     add_twin(7 - 4 * c, (2, 2))
-    send_last(2, 3, 4, 5, 6, 7)
+    send_last(3, 2, 4, 5, 6, 7)
     gather(4)
     gather(5)
     gather(6)

time: 55.9 us -> 57 us (1.020)
  the two profiles are of different devices: /device:TPU:203 before, /device:TPU:139 now
where the time goes in v6:
time: 57 us; the launch traced here: 56.9 us
  Pallas kernels  56.2 us (99%)
  local copies, waits for them, and re-layouts  0.6 us (1%)
    pallas_call x1, Pallas kernels, per_device(): pl.pallas_call(kernel, out_shape=jax.ShapeDtypeStruct((G, W), BF16), in_s...  56.2 us

profile of v6, /device:TPU:139, one launch (start us, length us, event | category | flops | bytes accessed | tf_op | source)
XLA Modules:
  0.0 56.9 jit_solution(552191754855839085)
XLA Ops:
  0.0 56.2 %shard_map.28 = bf16[48,128]{1,0:T(8,128)(2,1)S(1)} custom-call(bf16[2,4,48,1280]{3,2,1,0:T(8,128)(2,1)} %bitcast.1, bf16[1280,512]{1,0:T(8,128)(2,1)} %t_hbm.1), custom_call_target="tpu_custom_call" | custom-call | tf_op jit(solution)/shard_map/pallas_call | solution.py:265
  56.3 0.6 %copy.4 = bf16[48,128]{1,0:T(8,128)(2,1)} copy(bf16[48,128]{1,0:T(8,128)(2,1)S(1)} %shard_map.28) | data formatting | bytes 24576
